TPU v7x, 32 devices: a whole 2x2x4 slice. The times are simulated.
32 devices in a mesh: dp: 8 (over z, y), tp: 4 (over x, core).
Axes of the slice: x: 2, y: 2, z: 4, core: 2. Of those that a mesh axis runs over, the one named last changes fastest.
Arguments:
- inputs: bfloat16 [1024, 16, 768], P('tp', 'dp'), may hold values from -6 to 6
- lengths: int32 [16], P('dp'), may hold values from 256 to 1024, as said below
- w_query: bfloat16 [768, 768], P(None, 'tp'), may hold values from -0.21875 to 0.21875
- b_query: float32 [768], P('tp'), may hold values from -3 to 3
- w_key: bfloat16 [768, 768], P(None, 'tp'), may hold values from -0.21875 to 0.21875
- w_value: bfloat16 [768, 768], P(None, 'tp'), may hold values from -0.21875 to 0.21875
- b_value: float32 [768], P('tp'), may hold values from -0.2 to 0.2
- w_out: bfloat16 [768, 768], P('tp'), may hold values from -6 to 6
- b_out: float32 [768], replicated, may hold values from -3 to 3
- norm1_gain: float32 [768], replicated, may hold values from 0.5 to 1.5
- norm1_bias: float32 [768], replicated, may hold values from -2 to 2
- w_up: bfloat16 [768, 3072], P(None, 'tp'), may hold values from -0.21875 to 0.21875
- b_up: float32 [3072], P('tp'), may hold values from -3 to 3
- w_down: bfloat16 [3072, 768], P('tp'), may hold values from -0.109375 to 0.109375
- b_down: float32 [768], replicated, may hold values from -3 to 3
- norm2_gain: float32 [768], replicated, may hold values from 0.5 to 1.5
- norm2_bias: float32 [768], replicated, may hold values from -2 to 2
- cotangent: bfloat16 [1024, 16, 768], P('tp', 'dp'), may hold values from -6 to 6
Outputs:
- outputs: bfloat16 [1024, 16, 768], P('tp', 'dp')
- input_grad: float32 [1024, 16, 768], P('tp', 'dp')
- grad_w_query: float32 [768, 768], P(None, 'tp')
- grad_b_query: float32 [768], P('tp')
- grad_w_key: float32 [768, 768], P(None, 'tp')
- grad_w_value: float32 [768, 768], P(None, 'tp')
- grad_b_value: float32 [768], P('tp')
- grad_w_out: float32 [768, 768], P('tp')
- grad_b_out: float32 [768], replicated
- grad_norm1_gain: float32 [768], replicated
- grad_norm1_bias: float32 [768], replicated
- grad_w_up: float32 [768, 3072], P(None, 'tp')
- grad_b_up: float32 [3072], P('tp')
- grad_w_down: float32 [3072, 768], P('tp')
- grad_b_down: float32 [768], replicated
- grad_norm2_gain: float32 [768], replicated
- grad_norm2_bias: float32 [768], replicated
Inputs may be any that keep to these rules, and one draw needn't show every extreme that they name: Utterance b occupies its first lengths[b] slots; the rest are padding. Utterance 0 has exactly 1024 valid frames.
All inputs are finite; a program needn't handle non-finite values.
Results may differ from a plain program's by a relative error of at most 0.018.
Values may be sent and summed in bfloat16 or wider, within the bound.
A program may use at most 128 MiB of HBM per device.

v0:
```python
import jax
import jax.numpy as jnp
from jax import lax
from jax.sharding import PartitionSpec as P

HEAD_DIM = 64
MICRO = 2


EPS = 1e-05
ROOT_HALF = 0.7071067811865476
DENSITY = 0.3989422804014327
SCALE = 0.125


def normalize(value, gain, bias):
    centered = value - jnp.mean(value, -1, keepdims=True)
    inverse = lax.rsqrt(jnp.mean(centered * centered, -1, keepdims=True) + EPS)
    scaled = centered * inverse
    return (scaled * gain + bias, scaled, inverse)


def normalize_back(grad_out, gain, scaled, inverse):
    inner = grad_out * gain
    return inverse * (
        inner
        - jnp.mean(inner, -1, keepdims=True)
        - scaled * jnp.mean(inner * scaled, -1, keepdims=True)
    )


def gelu_slope(value):
    return 0.5 * (1.0 + lax.erf(value * ROOT_HALF)) + value * DENSITY * jnp.exp(
        -0.5 * value * value
    )


def rows_times(left, right):
    return jnp.dot(left, right, preferred_element_type=jnp.float32)


def rows_times_back(left, right):
    return jnp.einsum("rc,dc->rd", left, right, preferred_element_type=jnp.float32)


def block_scores(q_block, keys, mask):
    scores = (
        jnp.einsum("qbhe,kbhe->bhqk", q_block, keys, preferred_element_type=jnp.float32) * SCALE
    )
    return jnp.where(mask, scores, -jnp.inf)


def row_total(value):
    return jnp.sum(value.astype(jnp.float32), 0)


def local(
    inputs,
    lengths,
    w_query,
    b_query,
    w_key,
    w_value,
    b_value,
    w_out,
    b_out,
    norm1_gain,
    norm1_bias,
    w_up,
    b_up,
    w_down,
    b_down,
    norm2_gain,
    norm2_bias,
    cotangent,
):
    local_len, utt_dev, width = inputs.shape
    length = local_len * lax.axis_size("tp")
    local_cols = w_query.shape[1]
    heads_local = local_cols // HEAD_DIM
    per_batch = utt_dev // MICRO
    local_rows = local_len * per_batch
    all_rows = length * per_batch
    qblock = min(512, length)
    blocks = length // qblock
    w_three = jnp.concatenate([w_query, w_key, w_value], 1)
    b_three = jnp.concatenate([b_query, jnp.zeros_like(b_query), b_value])
    totals = (
        jnp.zeros(w_three.shape, jnp.float32),
        jnp.zeros(b_three.shape, jnp.float32),
        jnp.zeros(w_out.shape, jnp.float32),
        jnp.zeros(w_up.shape, jnp.float32),
        jnp.zeros(b_up.shape, jnp.float32),
        jnp.zeros(w_down.shape, jnp.float32),
    )
    norm_totals = tuple((jnp.zeros((width,), jnp.float32) for _ in range(6)))
    out_pieces = []
    grad_pieces = []
    for batch_index in range(MICRO):
        first = batch_index * per_batch
        x_part = inputs[:, first : first + per_batch].reshape(local_rows, width)
        lens_part = lengths[first : first + per_batch]
        tangent = (
            cotangent[:, first : first + per_batch].reshape(local_rows, width).astype(jnp.float32)
        )
        x_full = lax.all_gather(x_part, "tp", axis=0, tiled=True)
        projected = jnp.dot(x_full, w_three, preferred_element_type=jnp.float32) + b_three
        shape_heads = (length, per_batch, heads_local, HEAD_DIM)
        query = projected[:, :local_cols].astype(jnp.bfloat16).reshape(shape_heads)
        keys = projected[:, local_cols : 2 * local_cols].astype(jnp.bfloat16).reshape(shape_heads)
        values = projected[:, 2 * local_cols :].astype(jnp.bfloat16).reshape(shape_heads)
        valid = lax.broadcasted_iota(jnp.int32, (per_batch, length), 1) < lens_part[:, None]
        mask = valid[:, None, None, :]
        contexts = []
        log_totals = []
        for block_index in range(blocks):
            q_block = query[block_index * qblock : (block_index + 1) * qblock]
            scores = block_scores(q_block, keys, mask)
            top = jnp.max(scores, -1, keepdims=True)
            expo = jnp.exp(scores - top)
            total = jnp.sum(expo, -1, keepdims=True)
            probs = (expo / total).astype(jnp.bfloat16)
            log_totals.append(top + jnp.log(total))
            contexts.append(
                jnp.einsum("bhqk,kbhe->qbhe", probs, values, preferred_element_type=jnp.float32)
            )
        context_low = (
            jnp.concatenate(contexts, 0).astype(jnp.bfloat16).reshape(all_rows, local_cols)
        )
        attn_part = lax.psum_scatter(
            rows_times(context_low, w_out), "tp", scatter_dimension=0, tiled=True
        )
        hidden, scaled_one, inverse_one = normalize(
            x_part.astype(jnp.float32) + attn_part + b_out, norm1_gain, norm1_bias
        )
        hidden_low = hidden.astype(jnp.bfloat16)
        h_full = lax.all_gather(hidden_low, "tp", axis=0, tiled=True)
        upward = jnp.dot(h_full, w_up, preferred_element_type=jnp.float32) + b_up
        active = jax.nn.gelu(upward, approximate=False).astype(jnp.bfloat16)
        ffn_part = lax.psum_scatter(
            rows_times(active, w_down).astype(jnp.bfloat16), "tp", scatter_dimension=0, tiled=True
        ).astype(jnp.float32)
        result, scaled_two, inverse_two = normalize(
            hidden + ffn_part + b_down, norm2_gain, norm2_bias
        )
        out_pieces.append(result.astype(jnp.bfloat16).reshape(local_len, per_batch, width))
        x_full, h_full = (
            lax.all_gather(x_part, "tp", axis=0, tiled=True),
            lax.all_gather(hidden_low, "tp", axis=0, tiled=True),
        )
        grad_gain_two = jnp.sum(tangent * scaled_two, 0)
        grad_bias_two = jnp.sum(tangent, 0)
        grad_two = normalize_back(tangent, norm2_gain, scaled_two, inverse_two)
        grad_ffn = grad_two.astype(jnp.bfloat16)
        grad_b_down = row_total(grad_ffn)
        ffn_rows = lax.all_gather(grad_ffn, "tp", axis=0, tiled=True)
        grad_w_down = jnp.einsum("rf,rd->fd", active, ffn_rows, preferred_element_type=jnp.float32)
        grad_active = jnp.einsum("rd,fd->rf", ffn_rows, w_down, preferred_element_type=jnp.float32)
        grad_up = (grad_active * gelu_slope(upward)).astype(jnp.bfloat16)
        grad_b_up = row_total(grad_up)
        grad_w_up = jnp.einsum("rd,rf->df", h_full, grad_up, preferred_element_type=jnp.float32)
        grad_hidden = grad_two + lax.psum_scatter(
            rows_times_back(grad_up, w_up).astype(jnp.bfloat16),
            "tp",
            scatter_dimension=0,
            tiled=True,
        ).astype(jnp.float32)
        grad_gain_one = jnp.sum(grad_hidden * scaled_one, 0)
        grad_bias_one = jnp.sum(grad_hidden, 0)
        grad_one = normalize_back(grad_hidden, norm1_gain, scaled_one, inverse_one)
        grad_attn = grad_one.astype(jnp.bfloat16)
        grad_b_out = row_total(grad_attn)
        attn_rows = lax.all_gather(grad_attn, "tp", axis=0, tiled=True)
        grad_w_out = jnp.einsum(
            "rc,rd->cd", context_low, attn_rows, preferred_element_type=jnp.float32
        )
        grad_context = jnp.einsum("rd,cd->rc", attn_rows, w_out, preferred_element_type=jnp.float32)
        grad_context = grad_context.astype(jnp.bfloat16).reshape(shape_heads)
        grad_keys = jnp.zeros(shape_heads, jnp.float32)
        grad_values = jnp.zeros(shape_heads, jnp.float32)
        grad_queries = []
        for block_index in range(blocks):
            lower = block_index * qblock
            q_block = query[lower : lower + qblock]
            ctx_grad = grad_context[lower : lower + qblock]
            probs = jnp.exp(block_scores(q_block, keys, mask) - log_totals[block_index])
            probs_low = probs.astype(jnp.bfloat16)
            grad_probs = jnp.einsum(
                "qbhe,kbhe->bhqk", ctx_grad, values, preferred_element_type=jnp.float32
            )
            centre = jnp.sum(probs * grad_probs, -1, keepdims=True)
            grad_scores = (probs * (grad_probs - centre)).astype(jnp.bfloat16)
            grad_queries.append(
                (
                    jnp.einsum(
                        "bhqk,kbhe->qbhe", grad_scores, keys, preferred_element_type=jnp.float32
                    )
                    * SCALE
                ).astype(jnp.bfloat16)
            )
            grad_keys = (
                grad_keys
                + jnp.einsum(
                    "bhqk,qbhe->kbhe", grad_scores, q_block, preferred_element_type=jnp.float32
                )
                * SCALE
            )
            grad_values = grad_values + jnp.einsum(
                "bhqk,qbhe->kbhe", probs_low, ctx_grad, preferred_element_type=jnp.float32
            )
        grad_three = jnp.concatenate(
            [
                jnp.concatenate(grad_queries, 0).reshape(all_rows, local_cols),
                grad_keys.astype(jnp.bfloat16).reshape(all_rows, local_cols),
                grad_values.astype(jnp.bfloat16).reshape(all_rows, local_cols),
            ],
            1,
        )
        grad_w_three = jnp.einsum(
            "rd,rc->dc", x_full, grad_three, preferred_element_type=jnp.float32
        )
        grad_b_three = row_total(grad_three)
        grad_input = grad_one + lax.psum_scatter(
            rows_times_back(grad_three, w_three).astype(jnp.bfloat16),
            "tp",
            scatter_dimension=0,
            tiled=True,
        ).astype(jnp.float32)
        grad_pieces.append(grad_input.reshape(local_len, per_batch, width))
        batch_grads = (grad_w_three, grad_b_three, grad_w_out, grad_w_up, grad_b_up, grad_w_down)
        totals = tuple((left + right for left, right in zip(totals, batch_grads)))
        batch_norms = (
            grad_b_out,
            grad_gain_one,
            grad_bias_one,
            grad_b_down,
            grad_gain_two,
            grad_bias_two,
        )
        norm_totals = tuple((left + right for left, right in zip(norm_totals, batch_norms)))
    totals = lax.psum(totals, "dp")
    norm_totals = lax.psum(norm_totals, ("dp", "tp"))
    grad_w_three, grad_b_three, grad_w_out, grad_w_up, grad_b_up, grad_w_down = totals
    outputs = jnp.concatenate(out_pieces, 1)
    input_grad = jnp.concatenate(grad_pieces, 1)
    return (
        outputs,
        input_grad,
        grad_w_three[:, :local_cols],
        grad_b_three[:local_cols],
        grad_w_three[:, local_cols : 2 * local_cols],
        grad_w_three[:, 2 * local_cols :],
        grad_b_three[2 * local_cols :],
        grad_w_out,
        norm_totals[0],
        norm_totals[1],
        norm_totals[2],
        grad_w_up,
        grad_b_up,
        grad_w_down,
        norm_totals[3],
        norm_totals[4],
        norm_totals[5],
    )


def solution(mesh):
    return jax.shard_map(
        local,
        mesh=mesh,
        in_specs=(
            P("tp", "dp", None),
            P("dp"),
            P(None, "tp"),
            P("tp"),
            P(None, "tp"),
            P(None, "tp"),
            P("tp"),
            P("tp", None),
            P(),
            P(),
            P(),
            P(None, "tp"),
            P("tp"),
            P("tp", None),
            P(),
            P(),
            P(),
            P("tp", "dp", None),
        ),
        out_specs=(
            P("tp", "dp", None),
            P("tp", "dp", None),
            P(None, "tp"),
            P("tp"),
            P(None, "tp"),
            P(None, "tp"),
            P("tp"),
            P("tp", None),
            P(),
            P(),
            P(),
            P(None, "tp"),
            P("tp"),
            P("tp", None),
            P(),
            P(),
            P(),
        ),
        check_vma=False,
    )
```

profile of v0, /device:TPU:0, one launch (start us, length us, event | category | flops | bytes accessed | tf_op | source)
XLA Modules:
  0.0 752.9 jit_solution(12142838873959318204)
XLA Ops:
  7.3 2.9 fusion.143
  15.2 19.2 %all-gather.23.cloned.1.call-done = bf16[1024,1,768]{2,0,1:T(8,128)(2,1)} async-done(((bf16[256,1,768]{2,0,1:T(8,128)(2,1)}), bf16[1024,1,768]{2,0,1:T(8,128)(2,1)}) %all-gather.23.cloned.1.call-update) | async-done | bytes 1572880 | tf_op jit(solution)/shard_map/all_gather | solution.py:106
  34.4 2.8 fusion.62
  46.1 2.2 fusion.122
  49.3 6.9 all-gather.25.cloned.1.call-done
  56.2 2.5 fusion.65
  67.7 2.3 fusion.120
  70.1 26.7 %reduce-scatter.9.cloned.1.call-done = f32[256,768]{1,0:T(8,128)} async-done(((f32[1024,768]{1,0:T(8,128)}), f32[256,768]{1,0:T(8,128)}) %reduce-scatter.9.cloned.1.call-update) | async-done | bytes 786448 | tf_op jit(solution)/shard_map/reduce_scatter | solution.py:130
  96.8 40.6 %reduce-scatter.13.cloned.1.call-done = f32[256,768]{1,0:T(8,128)} async-done(((f32[1024,768]{1,0:T(8,128)}), f32[256,768]{1,0:T(8,128)}) %reduce-scatter.13.cloned.1.call-update) | async-done | bytes 786448 | tf_op jit(solution)/shard_map/reduce_scatter | solution.py:130
  142.8 19.0 %all-gather.13.cloned.1.call-done = bf16[1024,768]{1,0:T(8,128)(2,1)} async-done(((bf16[256,768]{1,0:T(8,128)(2,1)}), bf16[1024,768]{1,0:T(8,128)(2,1)}) %all-gather.13.cloned.1.call-update) | async-done | bytes 1572880 | tf_op jit(solution)/shard_map/all_gather | solution.py:137
  161.8 4.4 fusion.152
  166.2 17.3 %all-gather.11.cloned.1.call-done = bf16[1024,768]{1,0:T(8,128)(2,1)} async-done(((bf16[256,768]{1,0:T(8,128)(2,1)}), bf16[1024,768]{1,0:T(8,128)(2,1)}) %all-gather.11.cloned.1.call-update) | async-done | bytes 1572880 | tf_op jit(solution)/shard_map/all_gather | solution.py:137
  183.5 16.8 %fusion.10 = (bf16[1024,768]{1,0:T(8,128)(2,1)S(1)}, bf16[1024,768]{1,0:T(8,128)(2,1)}, f32[1024,768]{1,0:T(8,128)}) fusion(f32[768]{0:T(1024)} %param.30, f32[1024,768]{1,0:T(8,128)} %fusion.152, bf16[1024,768]{1,0:T(8,128)(2,1)} %all-gather.11.cloned.1.call-done, bf16[768,768]{1,0:T(8,128)(2,1)S(1)} %copy-done), kind=kOutput, calls=%fused_computation.38 | convolution fusion | flops 1311768576 | bytes 12192768 | tf_op jit(solution)/shard_map/dot_general | solution.py:138
  201.5 2.5 convolution_convert_fusion.5
  204.1 4.3 convolution_convert_fusion.4
  208.5 3.0 fusion.142
  213.1 19.3 %reduce-scatter.11.cloned.1.call-done = bf16[256,768]{1,0:T(8,128)(2,1)} async-done(((bf16[1024,768]{1,0:T(8,128)(2,1)}), bf16[256,768]{1,0:T(8,128)(2,1)}) %reduce-scatter.11.cloned.1.call-update) | async-done | bytes 393232 | tf_op jit(solution)/shard_map/reduce_scatter | solution.py:140
  232.4 31.4 %reduce-scatter.15.cloned.1.call-done = bf16[256,768]{1,0:T(8,128)(2,1)} async-done(((bf16[1024,768]{1,0:T(8,128)(2,1)}), bf16[256,768]{1,0:T(8,128)(2,1)}) %reduce-scatter.15.cloned.1.call-update) | async-done | bytes 393232 | tf_op jit(solution)/shard_map/reduce_scatter | solution.py:140
  267.5 2.9 convert_reduce_fusion.6
  271.5 18.8 %all-gather.15.cloned.1.call-done = bf16[1024,768]{1,0:T(8,128)(2,1)} async-done(((bf16[256,768]{1,0:T(8,128)(2,1)}), bf16[1024,768]{1,0:T(8,128)(2,1)}) %all-gather.15.cloned.1.call-update) | async-done | bytes 1572880 | tf_op jit(solution)/shard_map/all_gather | solution.py:156
  290.3 5.4 convert_reduce_fusion.1
  296.9 2.6 convolution_convert_fusion.3
  299.6 12.4 %all-gather.19.cloned.1.call-done = bf16[1024,768]{1,0:T(8,128)(2,1)} async-done(((bf16[256,768]{1,0:T(8,128)(2,1)}), bf16[1024,768]{1,0:T(8,128)(2,1)}) %all-gather.19.cloned.1.call-update) | async-done | bytes 1572880 | tf_op jit(solution)/shard_map/all_gather | solution.py:156
  312.0 5.4 convert_reduce_fusion
  318.6 2.6 convolution_convert_fusion.2
  321.3 22.0 %reduce-scatter.17.cloned.1.call-done = bf16[256,768]{1,0:T(8,128)(2,1)} async-done(((bf16[1024,768]{1,0:T(8,128)(2,1)}), bf16[256,768]{1,0:T(8,128)(2,1)}) %reduce-scatter.17.cloned.1.call-update) | async-done | bytes 393232 | tf_op jit(solution)/shard_map/reduce_scatter | solution.py:162
  343.3 2.3 multiply_reduce_fusion.5
  345.6 29.0 %reduce-scatter.21.cloned.1.call-done = bf16[256,768]{1,0:T(8,128)(2,1)} async-done(((bf16[1024,768]{1,0:T(8,128)(2,1)}), bf16[256,768]{1,0:T(8,128)(2,1)}) %reduce-scatter.21.cloned.1.call-update) | async-done | bytes 393232 | tf_op jit(solution)/shard_map/reduce_scatter | solution.py:162
  374.6 3.6 convert_reduce_fusion.9
  378.3 2.4 convert_reduce_fusion.8
  385.0 15.4 %all-gather.21.cloned.1.call-done = bf16[1024,768]{1,0:T(8,128)(2,1)} async-done(((bf16[256,768]{1,0:T(8,128)(2,1)}), bf16[1024,768]{1,0:T(8,128)(2,1)}) %all-gather.21.cloned.1.call-update) | async-done | bytes 1572880 | tf_op jit(solution)/shard_map/all_gather | solution.py:173
  402.7 3.9 multiply_reduce_fusion.1
  412.5 4.2 multiply_reduce_fusion
  416.7 5.4 all-gather.17.cloned.1.call-done
  425.0 4.1 fusion.78
  429.6 3.5 multiply_convert_fusion
  435.6 2.6 convolution_convert_fusion
  438.5 3.9 multiply_reduce_fusion.3
  455.2 2.6 convolution_convert_fusion.1
  458.2 3.5 fusion.156
  463.6 2.9 convolution_add_fusion
  466.6 2.9 convolution_add_fusion.1
  473.8 2.4 add_bitcast_fusion
  479.4 40.5 %all-reduce = (f32[768]{0:T(1024)}, f32[768]{0:T(1024)}, f32[768]{0:T(1024)}, f32[768]{0:T(1024)}, f32[768]{0:T(1024)}, /*index=5*/f32[768]{0:T(1024)}) all-reduce(f32[768]{0:T(1024)S(1)} %add.339, f32[768]{0:T(1024)S(1)} %add.340, f32[768]{0:T(1024)S(1)} %add.341, f32[768]{0:T(1024)S(1)} %add.345, ...), channel_id=1, replica_groups=mesh['dp'=8,'tp'=4] {'dp','tp'}, use_global_device_ids=true, to_apply=%region_43.44 | all-reduce | flops 4608 | bytes 36864 | tf_op jit(solution)/shard_map/psum | solution.py:242
  522.5 24.1 %all-reduce.1 = (f32[576]{0:T(1024)S(1)}, f32[768]{0:T(1024)}) all-reduce(f32[576]{0:T(1024)S(1)} %add.337, f32[768]{0:T(1024)S(1)} %add.343), channel_id=1, replica_groups=mesh['dp'=8,'tp'=4] {'dp'}, use_global_device_ids=true, to_apply=%region_39.40 | all-reduce | flops 1344 | bytes 10752 | tf_op jit(solution)/shard_map/psum | solution.py:241
  549.5 2.4 copy.40
  551.9 187.6 %all-reduce.5.cloned.1.call-done = (f32[768,576]{0,1:T(8,128)}, f32[192,768]{1,0:T(8,128)}, f32[768,768]{1,0:T(8,128)}, f32[768,768]{1,0:T(8,128)}) async-done(((f32[768,576]{0,1:T(8,128)}, f32[192,768]{1,0:T(8,128)}, f32[768,768]{1,0:T(8,128)}, f32[768,768]{1,0:T(8,128)}), (f32[768,576]{0,1:T(8,128)}, f32[192,768]{1,0:T(8,128)}, f32[768,768]{1,0:T(8,128)}, ...) | async-done | bytes 7077904 | tf_op jit(solution)/shard_map/psum | solution.py:241
  739.5 2.8 fusion.137
  (374 shorter events, 88.2 us)
Async XLA Ops:
  7.2 154.6 %copy-start = (bf16[768,768]{1,0:T(8,128)(2,1)S(1)}, bf16[768,768]{1,0:T(8,128)(2,1)}, u32[]{:S(2)}) copy-start(bf16[768,768]{1,0:T(8,128)(2,1)} %param.29) | copy-start | bytes 3538948
  7.2 5.6 copy-start.95
  7.2 6.8 copy-start.53
  7.2 6.9 copy-start.54
  7.2 6.9 copy-start.55
  7.2 27.1 %all-gather.23.cloned.1.call-start = ((), (), s32[]{:S(2)}) async-start(), calls=%async_computation.22 | async-start | bytes 1966080 | tf_op jit(solution)/shard_map/all_gather | solution.py:106
  10.2 27.0 %copy-start.10 = (bf16[256,1,768]{2,1,0:T(2,128)(2,1)}, bf16[256,1,768]{2,1,0:T(2,128)(2,1)S(1)}, u32[]{:S(2)}) copy-start(bf16[256,1,768]{2,1,0:T(2,128)(2,1)S(1)} %get-tuple-element.100) | copy-start | bytes 1179652
  10.2 4.9 copy-start.96
  10.2 4.9 copy-start.97
  11.9 44.3 %all-gather.25.cloned.1.call-start = ((), (), s32[]{:S(2)}) async-start(), calls=%async_computation.23 | async-start | bytes 1966080 | tf_op jit(solution)/shard_map/all_gather | solution.py:106
  12.7 84.1 %reduce-scatter.9.cloned.1.call-start = ((), (), s32[]{:S(2)}) async-start(), calls=%async_computation.8 | async-start | bytes 3932160 | tf_op jit(solution)/shard_map/reduce_scatter | solution.py:130
  39.6 4.7 copy-start.2
  39.6 4.7 copy-start.64
  46.1 10.1 %copy-start.61 = (bf16[768,576]{0,1:T(8,128)(2,1)S(1)}, bf16[768,576]{0,1:T(8,128)(2,1)}, u32[]{:S(2)}) copy-start(bf16[768,576]{0,1:T(8,128)(2,1)} %copy-done.60) | copy-start | bytes 2654212
  48.4 89.0 %reduce-scatter.13.cloned.1.call-start = ((), (), s32[]{:S(2)}) async-start(), calls=%async_computation.11 | async-start | bytes 3932160 | tf_op jit(solution)/shard_map/reduce_scatter | solution.py:130
  58.9 7.1 copy-start.12
  60.0 4.2 copy-start.5
  67.7 69.8 %copy-start.91 = (f32[768]{0:T(1024)S(1)}, f32[768]{0:T(1024)}, u32[]{:S(2)}) copy-start(f32[768]{0:T(1024)} %param.26) | copy-start | bytes 9220
  70.0 70.1 %copy-start.59 = (f32[768]{0:T(1024)S(1)}, f32[768]{0:T(1024)}, u32[]{:S(2)}) copy-start(f32[768]{0:T(1024)} %param.27) | copy-start | bytes 9220
  70.0 91.8 %all-gather.13.cloned.1.call-start = ((), (), s32[]{:S(2)}) async-start(), calls=%async_computation.12 | async-start | bytes 1966080 | tf_op jit(solution)/shard_map/all_gather | solution.py:137
  142.0 41.5 %all-gather.11.cloned.1.call-start = ((), (), s32[]{:S(2)}) async-start(), calls=%async_computation.9 | async-start | bytes 1966080 | tf_op jit(solution)/shard_map/all_gather | solution.py:137
  142.6 89.8 %reduce-scatter.11.cloned.1.call-start = ((), (), s32[]{:S(2)}) async-start(), calls=%async_computation.10 | async-start | bytes 1966080 | tf_op jit(solution)/shard_map/reduce_scatter | solution.py:140
  183.5 18.0 %copy-start.103 = (bf16[768,768]{1,0:T(8,128)(2,1)S(1)}, bf16[768,768]{1,0:T(8,128)(2,1)}, u32[]{:S(2)}) copy-start(bf16[768,768]{1,0:T(8,128)(2,1)} %param.31) | copy-start | bytes 3538948
  204.1 59.8 %reduce-scatter.15.cloned.1.call-start = ((), (), s32[]{:S(2)}) async-start(), calls=%async_computation.13 | async-start | bytes 1966080 | tf_op jit(solution)/shard_map/reduce_scatter | solution.py:140
  208.4 81.9 %all-gather.15.cloned.1.call-start = ((), (), s32[]{:S(2)}) async-start(), calls=%async_computation.14 | async-start | bytes 1966080 | tf_op jit(solution)/shard_map/all_gather | solution.py:156
  270.5 41.5 %all-gather.19.cloned.1.call-start = ((), (), s32[]{:S(2)}) async-start(), calls=%async_computation.18 | async-start | bytes 1966080 | tf_op jit(solution)/shard_map/all_gather | solution.py:156
  271.1 72.2 %reduce-scatter.17.cloned.1.call-start = ((), (), s32[]{:S(2)}) async-start(), calls=%async_computation.15 | async-start | bytes 1966080 | tf_op jit(solution)/shard_map/reduce_scatter | solution.py:162
  299.5 75.1 %reduce-scatter.21.cloned.1.call-start = ((), (), s32[]{:S(2)}) async-start(), calls=%async_computation.19 | async-start | bytes 1966080 | tf_op jit(solution)/shard_map/reduce_scatter | solution.py:162
  321.2 53.4 %copy-start.11 = (f32[256,768]{1,0:T(8,128)S(1)}, f32[256,768]{1,0:T(8,128)}, u32[]{:S(2)}) copy-start(f32[256,768]{1,0:T(8,128)} %get-tuple-element.66) | copy-start | bytes 2359300
  321.2 53.4 %copy-start.68 = (f32[256]{0:T(256)S(1)}, f32[256]{0:T(256)}, u32[]{:S(2)}) copy-start(f32[256]{0:T(256)} %copy-done.67) | copy-start | bytes 3076
  321.2 53.4 %copy-start.75 = (f32[256]{0:T(256)S(1)}, f32[256]{0:T(256)}, u32[]{:S(2)}) copy-start(f32[256]{0:T(256)} %copy-done.74) | copy-start | bytes 3076
  321.2 53.4 %copy-start.77 = (f32[256]{0:T(256)S(1)}, f32[256]{0:T(256)}, u32[]{:S(2)}) copy-start(f32[256]{0:T(256)} %copy-done.76) | copy-start | bytes 3076
  321.2 79.3 %all-gather.21.cloned.1.call-start = ((), (), s32[]{:S(2)}) async-start(), calls=%async_computation.20 | async-start | bytes 1966080 | tf_op jit(solution)/shard_map/all_gather | solution.py:173
  378.3 24.4 %copy-start.13 = (bf16[1024,192]{0,1:T(8,128)(2,1)S(1)}, bf16[1024,192]{0,1:T(8,128)(2,1)}, u32[]{:S(2)}) copy-start(bf16[1024,192]{0,1:T(8,128)(2,1)} %copy-done.12) | copy-start | bytes 1179652
  380.7 41.5 %all-gather.17.cloned.1.call-start = ((), (), s32[]{:S(2)}) async-start(), calls=%async_computation.16 | async-start | bytes 1966080 | tf_op jit(solution)/shard_map/all_gather | solution.py:173
  384.8 162.4 %reduce-scatter.23.cloned.1.call-start = ((), (), s32[]{:S(2)}) async-start(), calls=%async_computation.21 | async-start | bytes 1966080 | tf_op jit(solution)/shard_map/reduce_scatter | solution.py:223
  402.7 4.8 slice-start.3
  406.6 4.7 slice-start.6
  416.7 8.2 %copy-start.29 = (bf16[512,192]{0,1:T(8,128)(2,1)S(1)}, bf16[512,192]{0,1:T(8,128)(2,1)}, u32[]{:S(2)}) copy-start(bf16[512,192]{0,1:T(8,128)(2,1)} %copy-done.28) | copy-start | bytes 589828
  425.0 4.6 copy-start.6
  425.0 4.6 copy-start.58
  425.0 4.6 copy-start.69
  429.1 6.2 copy-start.30
  438.2 110.1 %reduce-scatter.19.cloned.1.call-start = ((), (), s32[]{:S(2)}) async-start(), calls=%async_computation.17 | async-start | bytes 1966080 | tf_op jit(solution)/shard_map/reduce_scatter | solution.py:223
  438.4 4.7 slice-start.1
  455.2 18.2 %copy-start.32 = (bf16[3,64,1024]{2,1,0:T(8,128)(2,1)}, bf16[3,64,1024]{2,1,0:T(8,128)(2,1)S(1)}, u32[]{:S(2)}) copy-start(bf16[3,64,1024]{2,1,0:T(8,128)(2,1)S(1)} %fusion.81) | copy-start | bytes 1179652
  457.9 281.6 %all-reduce.5.cloned.1.call-start = ((), (), s32[]{:S(2)}) async-start(), calls=%async_computation.24 | async-start | bytes 14155776 | tf_op jit(solution)/shard_map/psum | solution.py:241
  477.6 70.7 %copy-start.16 = (f32[256,768]{1,0:T(8,128)S(1)}, f32[256,768]{1,0:T(8,128)}, u32[]{:S(2)}) copy-start(f32[256,768]{1,0:T(8,128)} %get-tuple-element.75) | copy-start | bytes 2359300
  (87 other events, 205.3 us)
Sparse Core Ops, SparseCore 0:
  12.0 22.3 all-gather.22
  36.5 19.6 all-gather.24
  58.8 38.0 reduce-scatter.8
  99.4 37.9 reduce-scatter.12
  142.1 19.6 all-gather.12
  163.8 19.6 all-gather.10
  204.2 28.1 reduce-scatter.10
  235.7 28.1 reduce-scatter.14
  270.6 19.6 all-gather.14
  292.3 19.6 all-gather.18
  315.1 28.1 reduce-scatter.16
  346.4 28.1 reduce-scatter.20
  380.8 19.6 all-gather.20
  402.5 19.6 all-gather.16
  438.3 28.1 reduce-scatter.22
  469.1 28.6 reduce-scatter.18
  503.1 236.2 all-reduce.4
where the time goes:
time: 761 us; the launch traced here: 753 us
  waiting for transfers between devices  472 us (62%)
  matrix products  120 us (16%)
  blocking collectives  64.6 us (8%)
  other arithmetic  45 us (6%)
  local copies, waits for them, and re-layouts  32.5 us (4%)
  between operations  16 us (2%)
    psum x1, waiting for transfers between devices, local(): totals = lax.psum(totals, 'dp')  188 us
    reduce_scatter x2, waiting for transfers between devices, local(): lax.psum_scatter(rows_times(context_low, w_out), 'tp', scatter_dimension=...  67.3 us
    reduce_scatter x2, waiting for transfers between devices, local(): lax.psum_scatter(rows_times_back(grad_up, w_up).astype(jnp.bfloat16), 'tp...  51 us
    reduce_scatter x2, waiting for transfers between devices, local(): lax.psum_scatter(rows_times(active, w_down).astype(jnp.bfloat16), 'tp', s...  50.7 us
    psum x1, blocking collectives, local(): norm_totals = lax.psum(norm_totals, ('dp', 'tp'))  40.5 us
    all_gather x2, waiting for transfers between devices, local(): h_full = lax.all_gather(hidden_low, 'tp', axis=0, tiled=True)  36.2 us
    all_gather x2, waiting for transfers between devices, local(): ffn_rows = lax.all_gather(grad_ffn, 'tp', axis=0, tiled=True)  31.2 us
    all_gather x2, waiting for transfers between devices, local(): x_full = lax.all_gather(x_part, 'tp', axis=0, tiled=True)  26.1 us
  transfers between devices with their start and end apart: 17, of which 15 were waited for; matrix products, arithmetic and copies ran while one was open for 16% of the time, Pallas kernels for 0%

commit v1 on v0

v1 whole, which is shorter than its diff:
```python
import functools
import math

import jax
import jax.numpy as jnp
from jax import lax
from jax.experimental import pallas as pl
from jax.experimental.pallas import tpu as pltpu
from jax.sharding import PartitionSpec as P

HEAD_DIM = 64
EPS = 1e-05
ROOT_HALF = 0.7071067811865476
DENSITY = 0.3989422804014327
SCALE = 0.125
NEG = -1e30
F32 = jnp.float32
BF16 = jnp.bfloat16


def dn(a, b):
    return lax.dot_general(a, b, (((1,), (0,)), ((), ())), preferred_element_type=F32)


def dnt(a, b):
    return lax.dot_general(a, b, (((1,), (1,)), ((), ())), preferred_element_type=F32)


def dtn(a, b):
    return lax.dot_general(a, b, (((0,), (0,)), ((), ())), preferred_element_type=F32)


def split3(v):
    hi = v.astype(BF16).astype(F32)
    rest = v - hi
    mid = rest.astype(BF16).astype(F32)
    return hi, mid, rest - mid


def mean(v):
    return jnp.mean(v, -1, keepdims=True)


def col_sum(v):
    return jnp.sum(v, 0, keepdims=True)


def chunk_of(n):
    for c in (96, 64, 48, 32, 16):
        if n % c == 0:
            return c
    return n


class Plan:
    def __init__(self, block, width, head_cols, ff_local, dp):
        self.block = block
        self.slots = 4 * block
        self.own = 2 * block
        self.width = width
        self.head_cols = head_cols
        self.heads = head_cols // HEAD_DIM
        self.ff = ff_local
        self.dp = dp
        self.bits = dp.bit_length() - 1
        self.wide = max(width, ff_local, 3 * head_cols)
        dpb = list(range(self.bits))
        first = dpb[:1]
        rest = dpb[1:]
        self.streams = [
            ("down", ff_local, width, ["x"] + dpb),
            ("up", width, ff_local, first + ["x"] + rest),
            ("out", head_cols, width, ["x"] + dpb),
            ("qkv", width, 3 * head_cols, ["x"] + dpb),
        ]

    def stream_buffers(self, rows, order):
        shapes = []
        n, both = rows, 2
        for dim in order:
            if dim == "x":
                shapes.append((1, n))
                both = 1
            elif (n // 2) % 16 == 0:
                n //= 2
                shapes.append((both, n))
            else:
                shapes.append((both, n))
        return shapes


def layer(plan, names, *refs):
    r = dict(zip(names, refs))
    block, slots, own, width = plan.block, plan.slots, plan.own, plan.width
    hc, heads, ff, dpn, bits = plan.head_cols, plan.heads, plan.ff, plan.dp, plan.bits
    dp = lax.axis_index("dp")
    tp = lax.axis_index("tp")
    x = lax.div(tp, 2)
    c = lax.rem(tp, 2)
    ox = 1 - x
    bit = [lax.rem(lax.div(dp, 1 << b), 2) for b in range(bits)]
    part = {b: (dp + (1 << b) * (1 - 2 * bit[b]), tp) for b in range(bits)}
    part["x"] = (dp, lax.rem(tp + 2, 4))
    part["c"] = (dp, tp + 1 - 2 * c)
    mesh_id = pl.DeviceIdType.MESH

    ssem, rsem, lsem = r["ssem"], r["rsem"], r["lsem"]
    count = {"r": 0, "l": 0}
    pending = []

    def send(src, dst, who):
        i = count["r"]
        count["r"] += 1
        copy = pltpu.make_async_remote_copy(
            src_ref=src,
            dst_ref=dst,
            send_sem=ssem.at[i],
            recv_sem=rsem.at[i],
            device_id=part[who],
            device_id_type=mesh_id,
        )
        copy.start()
        pending.append(copy)
        return copy

    def done_send(copies):
        for copy in copies:
            copy.wait_send()
            pending[:] = [p for p in pending if p is not copy]

    def local(src, dst):
        i = count["l"]
        count["l"] += 1
        copy = pltpu.make_async_copy(src, dst, lsem.at[i])
        copy.start()
        return copy

    def mult(v, m=16):
        return pl.multiple_of(v, math.gcd(m, 128))

    def row(i):
        return pl.multiple_of(lax.rem(c * own + i * block, slots), block)

    own0 = pl.multiple_of(c * own, own)
    mine = pl.multiple_of(x * block, block)
    other = pl.multiple_of(ox * block, block)

    barrier = pltpu.get_barrier_semaphore()
    for who in part.values():
        pl.semaphore_signal(barrier, inc=1, device_id=who, device_id_type=mesh_id)
    pl.semaphore_wait(barrier, len(part))

    gbits = min(2, bits)
    parts = 1 << gbits
    piece = lax.rem(dp, parts)

    def weight_x(name):
        src, dst = r[name], r["W" + name]
        n = src.shape[0] // parts
        at = pl.ds(mult(piece * n, n), n)
        return [send(src.at[at], dst.at[x, at], "x")]

    def weight_hop(name):
        dst = r["W" + name]
        n = dst.shape[1] // parts
        at = pl.ds(mult(piece * n, n), n)
        return [send(dst.at[ox, at], dst.at[ox, at], b) for b in range(gbits)]

    def weight_far(name):
        if gbits < 2:
            return []
        dst = r["W" + name]
        n = dst.shape[1] // parts
        copies = []
        rows_lo = (n // 2) // 16 * 16
        for b in range(2):
            other_bit = 1 - b
            from_piece = piece + (1 << other_bit) * (1 - 2 * bit[other_bit])
            start, size = (0, rows_lo) if b == 0 else (rows_lo, n - rows_lo)
            if size:
                at = pl.ds(mult(from_piece * n + start, 16), size)
                copies.append(send(dst.at[ox, at], dst.at[ox, at], b))
        return copies

    def arrived(copies):
        for copy in copies:
            copy.wait_recv()

    xs = r["X"]
    local_x = local(r["xin"].at[x], xs.at[pl.ds(own0 + mine, block)])
    local_w = [local(r[name], r["W" + name].at[x]) for name in ("w3", "wo", "wu", "wd")]
    local_b = [local(r["svec"], r["B"].at[x]), local(r["rvec"], r["R"])]
    local_c = local(r["cin"].at[x], r["cot"].at[pl.ds(mine, block)])
    w3_x = weight_x("w3")
    b_x = [send(r["svec"], r["B"].at[x], "x")]
    x_x = send(r["xin"].at[ox], xs.at[pl.ds(own0 + mine, block)], "x")
    local_x.wait()
    at_mine = pl.ds(own0 + mine, block)
    x_c = [send(xs.at[at_mine], xs.at[at_mine], "c")]
    arrived(w3_x)
    w3_h = weight_hop("w3")
    x_x.wait_recv()
    at_other = pl.ds(own0 + other, block)
    x_c.append(send(xs.at[at_other], xs.at[at_other], "c"))
    late_x = {name: weight_x(name) for name in ("wo", "wu", "wd")}
    c_x = send(r["cin"].at[ox], r["cot"].at[pl.ds(mine, block)], "x")
    arrived(w3_h)
    w3_f = weight_far("w3")
    for copy in local_w + local_b:
        copy.wait()
    arrived(b_x)
    arrived(x_c)

    bias = r["B"]
    rep = r["R"]

    lane = lax.broadcasted_iota(jnp.int32, (block, HEAD_DIM), 1)
    valid = r["lens"][x]

    def project(s):
        w3 = r["Ww3"]
        b3 = bias[s, 0:1, : 3 * hc]

        @pl.loop(0, 4)
        def _(i):
            at = pl.ds(pl.multiple_of(i * block, block), block)
            y = dn(xs[at, :], w3[s]) + b3
            first = i * block + block * jnp.where(i == 1, 1, 0) - block * jnp.where(i == 2, 1, 0)
            slot = first + lax.broadcasted_iota(jnp.int32, (block, HEAD_DIM), 0)
            masked = jnp.where(slot < valid, 0.0, NEG)
            k_end = jnp.where(lane == 0, masked, jnp.where(lane < 4, 1.0, 0.0)).astype(BF16)
            q_end = jnp.where(lane == 0, 1.0, 0.0).astype(BF16)
            v_end = jnp.where(lane < 3, 1.0, 0.0).astype(BF16)
            for h in range(heads):
                hs = s * heads + h
                lo = h * HEAD_DIM
                r["QP"][hs, at, :HEAD_DIM] = (y[:, lo : lo + HEAD_DIM] * SCALE).astype(BF16)
                r["QP"][hs, at, HEAD_DIM:] = q_end
                lo += hc
                r["KP"][hs, at, :HEAD_DIM] = y[:, lo : lo + HEAD_DIM].astype(BF16)
                r["KP"][hs, at, HEAD_DIM:] = k_end
                lo += hc
                r["VP"][hs, at, :HEAD_DIM] = y[:, lo : lo + HEAD_DIM].astype(BF16)
                r["VP"][hs, at, HEAD_DIM:] = v_end

    def attend(s):
        @pl.loop(0, 4)
        def _(i):
            at = pl.ds(pl.multiple_of(i * block, block), block)
            for h in range(heads):
                hs = s * heads + h
                q = r["QP"][hs, at, :]
                score = dnt(q, r["KP"][hs])
                top = jnp.max(score, -1, keepdims=True)
                expo = jnp.exp(score - top).astype(BF16)
                o = dn(expo, r["VP"][hs])
                total = o[:, HEAD_DIM : HEAD_DIM + 1]
                r["C"][s, at, h * HEAD_DIM : (h + 1) * HEAD_DIM] = (
                    o[:, :HEAD_DIM] / total
                ).astype(BF16)
                hi, mid, low = split3(-(top + jnp.log(total)))
                r["QP"][hs, at, HEAD_DIM:] = jnp.where(
                    lane == 0,
                    1.0,
                    jnp.where(
                        lane == 1, hi, jnp.where(lane == 2, mid, jnp.where(lane == 3, low, 0.0))
                    ),
                ).astype(BF16)

    project(x)
    attend(x)
    arrived(w3_f)
    late_h = {}
    for name in ("wo", "wu", "wd"):
        arrived(late_x[name])
        late_h[name] = weight_hop(name)
    project(ox)
    attend(ox)
    late_f = {}
    for name in ("wo", "wu", "wd"):
        arrived(late_h[name])
        late_f[name] = weight_far(name)

    sbuf, rbuf = r["SB"], r["RB"]

    def exchange(partial):
        copies = []
        for i in range(2):
            sbuf[i] = partial(row(2 + i)).astype(BF16)
            copies.append(send(sbuf.at[i], rbuf.at[i], "c"))
        return copies

    def share(buf, i):
        at = pl.ds(row(i), block)
        return send(buf.at[at], buf.at[at], "c")

    sums = r["sums"]
    sums[...] = jnp.zeros_like(sums)

    def add_sum(k, v, n=None):
        n = v.shape[-1]
        sums[pl.ds(k, 1), :n] = sums[pl.ds(k, 1), :n] + v

    def attn_out(at0):
        at = pl.ds(at0, block)
        return dn(r["C"][0, at, :], r["Wwo"][0]) + dn(r["C"][1, at, :], r["Wwo"][1])

    arrived(late_f["wo"])
    ex = exchange(attn_out)
    hb_c = []
    for i in range(2):
        a = attn_out(row(i)) + rep[0:1, :width]
        ex[i].wait_recv()
        z = xs[pl.ds(row(i), block), :].astype(F32) + a + rbuf[i].astype(F32)
        z = z - mean(z)
        inv = lax.rsqrt(mean(z * z) + EPS)
        n1 = z * inv
        at = pl.ds(i * block, block)
        r["N1"][at, :] = n1
        r["INV"][at, :] = jnp.broadcast_to(inv, (block, 128))
        r["HB"][pl.ds(row(i), block), :] = (n1 * rep[1:2, :width] + rep[2:3, :width]).astype(BF16)
        hb_c.append(share(r["HB"], i))
    done_send(ex)

    def up(s, first, last):
        @pl.loop(first, last)
        def _(i):
            at = pl.ds(row(i), block)
            u = dn(r["HB"][at, :], r["Wwu"][s]) + bias[s, 1:2, :ff]
            cdf = 0.5 * (1.0 + lax.erf(u * ROOT_HALF))
            r["G"][s, at, :] = (u * cdf).astype(BF16)
            r["SL"][s, at, :] = (cdf + u * (DENSITY * jnp.exp(-0.5 * u * u))).astype(BF16)

    up(x, 0, 2)
    arrived(hb_c)
    up(x, 2, 4)
    arrived(late_f["wu"])
    up(ox, 0, 4)

    def ffn_out(at0):
        at = pl.ds(at0, block)
        return dn(r["G"][0, at, :], r["Wwd"][0]) + dn(r["G"][1, at, :], r["Wwd"][1])

    arrived(late_f["wd"])
    ex = exchange(ffn_out)
    local_c.wait()
    c_x.wait_recv()
    df_c = []
    for i in range(2):
        at = pl.ds(i * block, block)
        hidden = r["N1"][at, :] * rep[1:2, :width] + rep[2:3, :width]
        f = ffn_out(row(i)) + rep[3:4, :width]
        ex[i].wait_recv()
        z = hidden + f + rbuf[i].astype(F32)
        z = z - mean(z)
        inv = lax.rsqrt(mean(z * z) + EPS)
        n2 = z * inv
        r["OB"][at, :] = (n2 * rep[4:5, :width] + rep[5:6, :width]).astype(BF16)
        dy = r["cot"][at, :].astype(F32)
        add_sum(4, col_sum(dy * n2))
        add_sum(5, col_sum(dy))
        e2 = dy * rep[4:5, :width]
        dz = inv * (e2 - mean(e2) - n2 * mean(e2 * n2))
        r["DZ"][at, :] = dz
        df = dz.astype(BF16)
        add_sum(3, col_sum(df.astype(F32)))
        r["DF"][pl.ds(row(i), block), :] = df
        df_c.append(share(r["DF"], i))
    done_send(ex)
    out_x = send(r["OB"].at[pl.ds(other, block)], r["out"].at[x], "x")
    out_l = local(r["OB"].at[pl.ds(mine, block)], r["out"].at[x])

    def adder(dst, d, row0, src, sd, n):
        size = chunk_of(n)

        @pl.loop(0, n // size)
        def _(i):
            at = pl.ds(mult(row0 + i * size), size)
            got = src[sd, pl.ds(mult(i * size), size), :].astype(F32)
            dst[d, at, :] = (dst[d, at, :].astype(F32) + got).astype(BF16)

    def stream(name, rows, order):
        grad, final = r["G_" + name], r["F_" + name]
        row0, n, both = 0, rows, True
        halved = []
        for k, dim in enumerate(order):
            got = r["S_%s_%d" % (name, k)]
            if dim == "x":
                at = pl.ds(row0, n)
                copy = send(grad.at[ox, at], got.at[0], "x")
                yield
                copy.wait_recv()
                adder(grad, x, row0, got, 0, n)
                both = False
                continue
            half = (n // 2) % 16 == 0
            if half:
                n //= 2
                halved.append(dim)
                sent = mult(row0 + (1 - bit[dim]) * n)
                row0 = mult(row0 + bit[dim] * n)
            else:
                sent = row0
            at = pl.ds(sent, n)
            src = grad.at[:, at] if both else grad.at[x, at]
            copy = send(src, got if both else got.at[0], dim)
            yield
            copy.wait_recv()
            if not half:
                done_send([copy])
            if both:
                adder(grad, 0, row0, got, 0, n)
                adder(grad, 1, row0, got, 1, n)
            else:
                adder(grad, x, row0, got, 0, n)
        first = True
        keep = local(grad.at[x, pl.ds(row0, n)], final.at[pl.ds(row0, n)])
        for dim in reversed(halved):
            at = pl.ds(row0, n)
            copy = send(grad.at[x, at] if first else final.at[at], final.at[at], dim)
            first = False
            yield
            copy.wait_recv()
            if keep is not None:
                keep.wait()
                keep = None
            row0 = mult(row0 - bit[dim] * n)
            n *= 2
        if keep is not None:
            keep.wait()

    live = []

    def begin(name):
        for n_, rows, _, order in plan.streams:
            if n_ == name:
                gen = stream(name, rows, order)
                live.append(gen)
        advance(gen)

    def advance(gen=None):
        for g in [gen] if gen is not None else list(live):
            try:
                next(g)
            except StopIteration:
                live.remove(g)

    def slope(first, last):
        @pl.loop(first, last)
        def _(i):
            at = pl.ds(row(i), block)
            for s in range(2):
                da = dnt(r["DF"][at, :], r["Wwd"][s])
                du = da * r["SL"][s, at, :].astype(F32)
                add_sum(8 + s, col_sum(du))
                r["SL"][s, at, :] = du.astype(BF16)

    def weight_grad(dst, left, right):
        for s in range(2):
            cols = dst.shape[1]
            size = min(256, cols)

            @pl.loop(0, cols // size)
            def _(j):
                at = pl.ds(pl.multiple_of(j * size, size), size)
                dst[s, at, :] = dtn(left(s, at), right(s)).astype(BF16)

    slope(0, 2)
    arrived(df_c)
    weight_grad(r["G_down"], lambda s, at: r["G"][s, :, at], lambda s: r["DF"][...])
    begin("down")
    slope(2, 4)
    weight_grad(r["G_up"], lambda s, at: r["HB"][:, at], lambda s: r["SL"][s])
    begin("up")

    def hidden_back(at0):
        at = pl.ds(at0, block)
        return dnt(r["SL"][0, at, :], r["Wwu"][0]) + dnt(r["SL"][1, at, :], r["Wwu"][1])

    ex = exchange(hidden_back)
    da_c = []
    for i in range(2):
        at = pl.ds(i * block, block)
        dh = r["DZ"][at, :] + hidden_back(row(i))
        ex[i].wait_recv()
        dh = dh + rbuf[i].astype(F32)
        n1 = r["N1"][at, :]
        add_sum(1, col_sum(dh * n1))
        add_sum(2, col_sum(dh))
        e1 = dh * rep[1:2, :width]
        dz = r["INV"][at, 0:1] * (e1 - mean(e1) - n1 * mean(e1 * n1))
        r["DZ"][at, :] = dz
        da = dz.astype(BF16)
        add_sum(0, col_sum(da.astype(F32)))
        r["DA"][pl.ds(row(i), block), :] = da
        da_c.append(share(r["DA"], i))
    done_send(ex)

    def context_back(first, last):
        @pl.loop(first, last)
        def _(i):
            at = pl.ds(row(i), block)
            for s in range(2):
                dc = dnt(r["DA"][at, :], r["Wwo"][s]).astype(BF16)
                for h in range(heads):
                    cols = slice(h * HEAD_DIM, (h + 1) * HEAD_DIM)
                    part_dc = dc[:, cols]
                    ctx = r["C"][s, at, cols].astype(F32)
                    hi, mid, low = split3(
                        -jnp.sum(part_dc.astype(F32) * ctx, -1, keepdims=True)
                    )
                    hs = s * heads + h
                    r["DC"][hs, at, :HEAD_DIM] = part_dc
                    r["DC"][hs, at, HEAD_DIM:] = jnp.where(
                        lane == 0,
                        hi,
                        jnp.where(lane == 1, mid, jnp.where(lane == 2, low, 0.0)),
                    ).astype(BF16)

    context_back(0, 2)
    arrived(da_c)
    context_back(2, 4)
    for s in range(2):
        r["G_out"][s] = dtn(r["C"][s], r["DA"][...]).astype(BF16)
    begin("out")

    acc_k, acc_v = r["AK"], r["AV"]

    def head_back(s, h):
        hs = s * heads + h

        @pl.loop(0, 4)
        def _(i):
            at = pl.ds(pl.multiple_of(i * block, block), block)
            q = r["QP"][hs, at, :]
            dc = r["DC"][hs, at, :]
            p = jnp.exp(dnt(r["KP"][hs], q))
            ds = (p * dnt(r["VP"][hs], dc)).astype(BF16)
            dv = dn(p.astype(BF16), dc)
            dk = dn(ds, q)
            dq = dtn(ds, r["KP"][hs])
            r["D3"][s, at, h * HEAD_DIM : (h + 1) * HEAD_DIM] = (
                dq[:, :HEAD_DIM] * SCALE
            ).astype(BF16)

            @pl.when(i == 0)
            def _():
                acc_k[...] = dk
                acc_v[...] = dv

            @pl.when(i > 0)
            def _():
                acc_k[...] = acc_k[...] + dk
                acc_v[...] = acc_v[...] + dv

        lo = hc + h * HEAD_DIM
        r["D3"][s, :, lo : lo + HEAD_DIM] = acc_k[:, :HEAD_DIM].astype(BF16)
        lo += hc
        r["D3"][s, :, lo : lo + HEAD_DIM] = acc_v[:, :HEAD_DIM].astype(BF16)

    for h in range(heads):

        @pl.loop(0, 2)
        def _(s):
            head_back(s, h)

        advance()

    for s in range(2):
        add_sum(10 + s, col_sum(r["D3"][s].astype(F32)))
    weight_grad(r["G_qkv"], lambda s, at: xs[:, at], lambda s: r["D3"][s])
    begin("qkv")

    def input_back(at0):
        at = pl.ds(at0, block)
        return dnt(r["D3"][0, at, :], r["Ww3"][0]) + dnt(r["D3"][1, at, :], r["Ww3"][1])

    ex = exchange(input_back)
    for i in range(2):
        at = pl.ds(i * block, block)
        dx = r["DZ"][at, :] + input_back(row(i))
        ex[i].wait_recv()
        r["DZ"][at, :] = dx + rbuf[i].astype(F32)
    r["DXS"][...] = r["DZ"][pl.ds(other, block), :].astype(BF16)
    dx_x = send(r["DXS"], r["dx_far"], "x")
    dx_l = local(r["DZ"].at[pl.ds(mine, block)], r["dx_own"])

    for k, who in enumerate(["c", "x"] + list(range(bits))):
        rows = 8 if who == "c" else 16
        copy = send(sums.at[pl.ds(0, rows)], r["SR"].at[k, pl.ds(0, rows)], who)
        advance()
        copy.wait_recv()
        done_send([copy])
        sums[0:rows, :] = sums[0:rows, :] + r["SR"][k, 0:rows, :]
    r["vec"][...] = sums[...]
    while live:
        advance()
    out_x.wait_recv()
    dx_x.wait_recv()
    out_l.wait()
    dx_l.wait()
    done_send(list(pending))


def local(
    inputs,
    lengths,
    w_query,
    b_query,
    w_key,
    w_value,
    b_value,
    w_out,
    b_out,
    norm1_gain,
    norm1_bias,
    w_up,
    b_up,
    w_down,
    b_down,
    norm2_gain,
    norm2_bias,
    cotangent,
):
    block, utts, width = inputs.shape
    dpn = lax.axis_size("dp")
    plan = Plan(block, width, w_query.shape[1], w_up.shape[1], dpn)
    hc, ff, wide = plan.head_cols, plan.ff, plan.wide
    slots, own, heads = plan.slots, plan.own, plan.heads

    xin = jnp.transpose(inputs, (1, 0, 2))
    cin = jnp.transpose(cotangent, (1, 0, 2))
    w3 = jnp.concatenate([w_query, w_key, w_value], 1)

    def rows_of(vectors):
        padded = [jnp.pad(v, (0, wide - v.shape[0])) for v in vectors]
        padded += [jnp.zeros((wide,), F32)] * (8 - len(padded))
        return jnp.stack(padded)

    b3 = jnp.concatenate([b_query, jnp.zeros_like(b_query), b_value])
    svec = rows_of([b3, b_up])
    rvec = rows_of([b_out, norm1_gain, norm1_bias, b_down, norm2_gain, norm2_bias])

    operands = [
        ("xin", xin),
        ("cin", cin),
        ("lens", lengths),
        ("w3", w3),
        ("wo", w_out),
        ("wu", w_up),
        ("wd", w_down),
        ("svec", svec),
        ("rvec", rvec),
    ]
    shape_of = jax.ShapeDtypeStruct
    hbm = pl.BlockSpec(memory_space=pl.ANY)
    vmem = pl.BlockSpec(memory_space=pltpu.VMEM)
    smem = pl.BlockSpec(memory_space=pltpu.SMEM)
    outs = [
        ("out", shape_of((2, block, width), BF16), hbm),
        ("dx_own", shape_of((block, width), F32), hbm),
        ("dx_far", shape_of((block, width), BF16), hbm),
        ("vec", shape_of((16, wide), F32), vmem),
    ]
    for name, rows, cols, _ in plan.streams:
        outs.append(("F_" + name, shape_of((rows, cols), BF16), vmem))

    def v(name, shape, dtype=BF16):
        return (name, pltpu.VMEM(shape, dtype))

    scratch = [
        v("X", (slots, width)),
        v("Ww3", (2, width, 3 * hc)),
        v("Wwo", (2, hc, width)),
        v("Wwu", (2, width, ff)),
        v("Wwd", (2, ff, width)),
        v("B", (2, 8, wide), F32),
        v("R", (8, wide), F32),
        v("cot", (own, width)),
        v("QP", (2 * heads, slots, 128)),
        v("KP", (2 * heads, slots, 128)),
        v("VP", (2 * heads, slots, 128)),
        v("DC", (2 * heads, slots, 128)),
        v("C", (2, slots, hc)),
        v("SB", (2, block, width)),
        v("RB", (2, block, width)),
        v("N1", (own, width), F32),
        v("INV", (own, 128), F32),
        v("HB", (slots, width)),
        v("G", (2, slots, ff)),
        v("SL", (2, slots, ff)),
        v("OB", (own, width)),
        v("DZ", (own, width), F32),
        v("DF", (slots, width)),
        v("DA", (slots, width)),
        v("D3", (2, slots, 3 * hc)),
        v("AK", (slots, 128), F32),
        v("AV", (slots, 128), F32),
        v("DXS", (block, width)),
        v("sums", (16, wide), F32),
        v("SR", (2 + plan.bits, 16, wide), F32),
    ]
    for name, rows, cols, order in plan.streams:
        scratch.append(v("G_" + name, (2, rows, cols)))
        for k, (both, n) in enumerate(plan.stream_buffers(rows, order)):
            scratch.append(v("S_%s_%d" % (name, k), (both, n, cols)))
    scratch += [
        ("ssem", pltpu.SemaphoreType.DMA((96,))),
        ("rsem", pltpu.SemaphoreType.DMA((96,))),
        ("lsem", pltpu.SemaphoreType.DMA((24,))),
    ]
    names = [n for n, _ in operands] + [n for n, _, _ in outs] + [n for n, _ in scratch]
    results = pl.pallas_call(
        functools.partial(layer, plan, names),
        out_shape=[s for _, s, _ in outs],
        in_specs=[smem if n == "lens" else hbm for n, _ in operands],
        out_specs=[s for _, _, s in outs],
        scratch_shapes=[s for _, s in scratch],
        compiler_params=pltpu.CompilerParams(
            collective_id=0, has_side_effects=True, vmem_limit_bytes=63 * 2**20
        ),
        name="encoder_layer",
    )(*[a for _, a in operands])
    got = dict(zip([n for n, _, _ in outs], results))
    first = lax.axis_index("tp") < 2
    near, far = got["dx_own"], got["dx_far"].astype(F32)
    input_grad = jnp.stack([jnp.where(first, near, far), jnp.where(first, far, near)], 1)
    outputs = jnp.transpose(got["out"], (1, 0, 2))
    vec = got["vec"]
    grad_b_up = jnp.where(first, vec[8], vec[9])[:ff]
    grad_b3 = jnp.where(first, vec[10], vec[11])
    qkv = got["F_qkv"].astype(F32)
    return (
        outputs,
        input_grad,
        qkv[:, :hc],
        grad_b3[:hc],
        qkv[:, hc : 2 * hc],
        qkv[:, 2 * hc :],
        grad_b3[2 * hc : 3 * hc],
        got["F_out"].astype(F32),
        vec[0, :width],
        vec[1, :width],
        vec[2, :width],
        got["F_up"].astype(F32),
        grad_b_up,
        got["F_down"].astype(F32),
        vec[3, :width],
        vec[4, :width],
        vec[5, :width],
    )


def solution(mesh):
    whole = P()
    rows = P("tp", "dp", None)
    cols = P(None, "tp")
    down = P("tp", None)
    shard = P("tp")
    return jax.shard_map(
        local,
        mesh=mesh,
        in_specs=(
            rows,
            P("dp"),
            cols,
            shard,
            cols,
            cols,
            shard,
            down,
            whole,
            whole,
            whole,
            cols,
            shard,
            down,
            whole,
            whole,
            whole,
            rows,
        ),
        out_specs=(
            rows,
            rows,
            cols,
            shard,
            cols,
            cols,
            shard,
            down,
            whole,
            whole,
            whole,
            cols,
            shard,
            down,
            whole,
            whole,
            whole,
        ),
        check_vma=False,
    )
```

time: 761 us -> 242 us (0.32); the launches traced: 753 us -> 242 us
  waiting for transfers between devices: 472 us -> 0 us
  Pallas kernels: 0 us -> 220 us
  matrix products: 120 us -> 0 us
  blocking collectives: 64.6 us -> 0 us
  other arithmetic: 45 us -> 8.16 us
  local copies, waits for them, and re-layouts: 32.5 us -> 12.3 us
  between operations: 16 us -> 0.94 us
    pallas_call x0 -> x1, Pallas kernels: none -> 220 us  [local(): pl.pallas_call(functools.partial(layer, plan, names), out_shape=[s for _,...]
    psum x1 -> x0, waiting for transfers between devices: 188 us -> none  [local(): totals = lax.psum(totals, 'dp')]
    reduce_scatter x8 -> x0, waiting for transfers between devices: 169 us -> none  [the longest x2 67.3 us: local(): lax.psum_scatter(rows_times(context_low, w_out), 'tp', scatter_dimension=...]
    dot_general x48 -> x0, matrix products: 120 us -> none  [the longest x2 21.3 us: local(): upward = jnp.dot(h_full, w_up, preferred_element_type=jnp.float32) + b_up]
    all_gather x8 -> x0, waiting for transfers between devices: 114 us -> none  [the longest x2 36.2 us: local(): h_full = lax.all_gather(hidden_low, 'tp', axis=0, tiled=True)]
    psum x2 -> x0, blocking collectives: 64.6 us -> none  [the longest x1 40.5 us: local(): norm_totals = lax.psum(norm_totals, ('dp', 'tp'))]
    reduce_sum x17 -> x0, other arithmetic: 27.5 us -> none  [the longest x5 11.6 us: row_total(): return jnp.sum(value.astype(jnp.float32), 0)]
    unnamed x245 -> x44, local copies, waits for them, and re-layouts: 21.8 us -> 7.92 us
  transfers between devices with their start and end apart: 17 -> 0, of which waited for: 15 -> 0; matrix products, arithmetic and copies ran while one was open for 16% -> 0% of each run, Pallas kernels for 0% -> 0%
where the time goes in v1:
time: 242 us
  Pallas kernels  220 us (91%)
  local copies, waits for them, and re-layouts  12.3 us (5%)
  other arithmetic  8.16 us (3%)
    pallas_call x1, Pallas kernels, local(): pl.pallas_call(functools.partial(layer, plan, names), out_shape=[s for _,...  220 us
    unnamed x44, local copies, waits for them, and re-layouts  7.92 us

profile of v1, /device:TPU:0, one launch (start us, length us, event | category | flops | bytes accessed | tf_op | source)
XLA Modules:
  0.0 241.8 jit_solution(9691587419476509649)
XLA Ops:
  0.7 0.0 copy-start.9
  0.7 0.0 copy-start.10
  0.7 0.0 copy-start.11
  0.7 0.0 copy-start.12
  0.7 0.0 copy-start.13
  0.7 0.0 copy-start.14
  0.7 0.0 copy-start.17
  0.7 0.0 copy-start.16
  0.7 0.0 copy-start.15
  0.8 0.0 copy-start.5
  0.8 0.0 copy-start.6
  0.8 0.0 copy-start.7
  0.8 2.8 %copy_bitcast_fusion = (bf16[2,256,768]{2,1,0:T(8,128)(2,1)}, bf16[2,256,768]{2,1,0:T(8,128)(2,1)}) fusion(bf16[256,2,768]{2,1,0:T(2,128)(2,1)} %param.35, bf16[256,2,768]{2,1,0:T(2,128)(2,1)} %param.18), kind=kLoop, calls=%fused_computation.6 | loop fusion | bytes 3145728 | tf_op jit(solution)/shard_map/transpose | solution.py:632
  3.6 0.0 copy-done.9
  3.6 0.0 copy-done.10
  3.6 0.0 copy-done.11
  3.6 0.0 copy-done.12
  3.6 0.0 copy-done.13
  3.7 0.0 copy-done.14
  3.7 0.6 stack.52.refs_8_
  4.3 0.1 select_maximum_fusion
  4.4 0.0 copy-done.15
  4.4 0.1 pad.10.clone
  4.5 0.7 maximum_maximum_fusion.refs_7_
  5.2 0.2 copy.37
  5.4 0.0 copy-done.6
  5.4 0.2 copy.38
  5.6 0.2 copy.39
  5.8 1.3 pad_maximum_fusion.1.refs_3_
  7.0 220.4 %encoder_layer.1 = (bf16[2,256,768]{2,1,0:T(8,128)(2,1)}, f32[256,768]{1,0:T(8,128)}, bf16[256,768]{1,0:T(8,128)(2,1)}, f32[16,768]{1,0:T(8,128)}, bf16[768,768]...) custom-call(bf16[2,256,768]{2,1,0:T(8,128)(2,1)} %get-tuple-element.66.refs_0_, ...), custom_call_target="tpu_custom_call" | custom-call | tf_op jit(solution)/shard_map/encoder_layer/pallas_call | solution.py:713
  227.4 1.3 fusion
  228.8 0.1 pad_maximum_fusion
  228.9 0.0 copy-start.8
  228.9 0.0 copy-start
  228.9 2.4 copy.41
  231.3 0.7 slice_reduce_fusion
  231.9 0.6 fusion.4
  232.5 0.3 fusion.3
  232.8 1.1 copy.42
  233.8 1.1 copy.43
  234.9 1.1 copy.44
  236.0 1.6 convert_element_type.20
  237.6 0.1 copy-done.1
  237.7 1.6 convert_element_type.21
  239.2 0.0 copy-done.3
  239.2 1.7 copy.40
  240.9 0.0 copy-done.4
  240.9 0.9 convert_element_type.19
  (22 shorter events, 0.1 us)
Async XLA Ops:
  0.7 2.9 %copy-start.9 = (f32[768]{0:T(1024)S(1)}, f32[768]{0:T(1024)}, u32[]{:S(2)}) copy-start(f32[768]{0:T(1024)} %param.26) | copy-start | bytes 9220
  0.7 2.9 %copy-start.10 = (f32[768]{0:T(1024)S(1)}, f32[768]{0:T(1024)}, u32[]{:S(2)}) copy-start(f32[768]{0:T(1024)} %param.27) | copy-start | bytes 9220
  0.7 2.9 %copy-start.11 = (f32[768]{0:T(1024)S(1)}, f32[768]{0:T(1024)}, u32[]{:S(2)}) copy-start(f32[768]{0:T(1024)} %param.28) | copy-start | bytes 9220
  0.7 2.9 %copy-start.12 = (f32[768]{0:T(1024)S(1)}, f32[768]{0:T(1024)}, u32[]{:S(2)}) copy-start(f32[768]{0:T(1024)} %param.32) | copy-start | bytes 9220
  0.7 2.9 %copy-start.13 = (f32[768]{0:T(1024)S(1)}, f32[768]{0:T(1024)}, u32[]{:S(2)}) copy-start(f32[768]{0:T(1024)} %param.33) | copy-start | bytes 9220
  0.7 3.0 %copy-start.14 = (f32[768]{0:T(1024)S(1)}, f32[768]{0:T(1024)}, u32[]{:S(2)}) copy-start(f32[768]{0:T(1024)} %param.34) | copy-start | bytes 9220
  0.7 3.6 %copy-start.17 = (f32[192]{0:T(256)S(1)}, f32[192]{0:T(256)}, u32[]{:S(2)}) copy-start(f32[192]{0:T(256)} %param.21) | copy-start | bytes 2308
  0.7 3.6 %copy-start.16 = (f32[192]{0:T(256)S(1)}, f32[192]{0:T(256)}, u32[]{:S(2)}) copy-start(f32[192]{0:T(256)} %param.24) | copy-start | bytes 2308
  0.7 3.7 %copy-start.15 = (f32[768]{0:T(1024)S(1)}, f32[768]{0:T(1024)}, u32[]{:S(2)}) copy-start(f32[768]{0:T(1024)} %param.30) | copy-start | bytes 9220
  0.8 4.5 %copy-start.5 = (bf16[768,192]{0,1:T(8,128)(2,1)S(1)}, bf16[768,192]{0,1:T(8,128)(2,1)}, u32[]{:S(2)}) copy-start(bf16[768,192]{0,1:T(8,128)(2,1)} %param.20) | copy-start | bytes 884740
  0.8 4.6 %copy-start.6 = (bf16[768,192]{0,1:T(8,128)(2,1)S(1)}, bf16[768,192]{0,1:T(8,128)(2,1)}, u32[]{:S(2)}) copy-start(bf16[768,192]{0,1:T(8,128)(2,1)} %param.22) | copy-start | bytes 884740
  0.8 4.8 %copy-start.7 = (bf16[768,192]{0,1:T(8,128)(2,1)S(1)}, bf16[768,192]{0,1:T(8,128)(2,1)}, u32[]{:S(2)}) copy-start(bf16[768,192]{0,1:T(8,128)(2,1)} %param.23) | copy-start | bytes 884740
  228.9 2.4 copy-start.8
  228.9 3.6 %copy-start = (bf16[768,576]{1,0:T(8,128)(2,1)S(1)}, bf16[768,576]{1,0:T(8,128)(2,1)}, u32[]{:S(2)}) copy-start(bf16[768,576]{1,0:T(8,128)(2,1)} %get-tuple-element.28) | copy-start | bytes 2654212
  233.8 2.1 copy-start.2
  236.0 1.7 copy-start.1
  237.7 1.6 copy-start.3
  239.2 1.7 copy-start.4
